TPU v7x, 256 devices: a whole 4x4x8 slice. The times are simulated.
256 devices in a mesh: fsdp: 32 (over x, z_hi, y), tensor: 8 (over z_lo, core).
Axes of the slice: x: 4, y: 4, z: 8 (z_hi: 2, z_lo: 4; z = z_hi * 4 + z_lo), core: 2. Of those that a mesh axis runs over, the one named last changes fastest.
Arguments:
- coeffs: bfloat16 [32768, 512], P('fsdp'), may hold values from -6 to 6
- pca_basis: bfloat16 [8192, 512], P('fsdp'), may hold values from -0.25 to 0.25
- w_gate: bfloat16 [8192, 14336], P('fsdp', 'tensor'), may hold values from -0.0625 to 0.0625
- w_up: bfloat16 [8192, 14336], P('fsdp', 'tensor'), may hold values from -0.0625 to 0.0625
- grad_hidden: bfloat16 [32768, 14336], P('fsdp', 'tensor'), may hold values from -1.1953125 to 1.1953125
Outputs:
- grad_coeffs: bfloat16 [32768, 512], P(('fsdp', 'tensor'))
- gate_grad_core: float32 [512, 14336], P('fsdp', 'tensor')
- up_grad_core: float32 [512, 14336], P('fsdp', 'tensor')
All inputs are finite; a program needn't handle non-finite values.
Results may differ from a plain program's by a relative error of at most 0.03.
Values may be sent and summed in bfloat16 or wider, within the bound.
No kernel may reach another device: no remote copies, remote signals or barrier semaphores. Data moves between devices by JAX's collectives and lax.ppermute only.
A program may use at most 64 MiB of HBM per device.

v0:
```python
import math

import jax
import jax.numpy as jnp
from jax import lax
from jax.sharding import PartitionSpec as P


def reduce_cores(gate_part, up_part):
    summed = lax.psum((gate_part, up_part), "fsdp")
    return (summed[0].astype(jnp.bfloat16), summed[1].astype(jnp.bfloat16))


def local(coeffs, pca_basis, w_gate, w_up, grad_hidden):
    gate_part = jnp.einsum("dr,df->rf", pca_basis, w_gate, preferred_element_type=jnp.float32)
    up_part = jnp.einsum("dr,df->rf", pca_basis, w_up, preferred_element_type=jnp.float32)
    gate_core, up_core = reduce_cores(gate_part, up_part)
    gate = jnp.dot(coeffs, gate_core, preferred_element_type=jnp.float32)
    upward = jnp.dot(coeffs, up_core, preferred_element_type=jnp.float32)
    sigmoid_gate = jax.nn.sigmoid(gate)
    grad_gate = (grad_hidden * upward * sigmoid_gate * (1.0 + gate * (1.0 - sigmoid_gate))).astype(
        jnp.bfloat16
    )
    grad_up = (grad_hidden * (gate * sigmoid_gate)).astype(jnp.bfloat16)
    token_scale = 1.0 / math.sqrt(coeffs.shape[0] * lax.axis_size("fsdp"))
    contract = (((1,), (1,)), ((), ()))
    total = lax.dot_general(grad_gate, gate_core, contract, preferred_element_type=jnp.float32)
    grad_coeffs = lax.psum_scatter(
        (
            total + lax.dot_general(grad_up, up_core, contract, preferred_element_type=jnp.float32)
        ).astype(jnp.bfloat16),
        "tensor",
        scatter_dimension=0,
        tiled=True,
    )
    contract = (((0,), (0,)), ((), ()))
    gate_term = (
        lax.dot_general(coeffs, grad_gate, contract, preferred_element_type=jnp.float32)
        * token_scale
    )
    up_term = (
        lax.dot_general(coeffs, grad_up, contract, preferred_element_type=jnp.float32) * token_scale
    )
    return (
        grad_coeffs,
        lax.psum_scatter(
            gate_term.astype(jnp.bfloat16), "fsdp", scatter_dimension=0, tiled=True
        ).astype(jnp.float32),
        lax.psum_scatter(
            up_term.astype(jnp.bfloat16), "fsdp", scatter_dimension=0, tiled=True
        ).astype(jnp.float32),
    )


def solution(mesh):
    placed = (
        P("fsdp", None),
        P("fsdp", None),
        P("fsdp", "tensor"),
        P("fsdp", "tensor"),
        P("fsdp", "tensor"),
    )
    return jax.shard_map(
        local,
        mesh=mesh,
        in_specs=placed,
        out_specs=(P(("fsdp", "tensor"), None), P("fsdp", "tensor"), P("fsdp", "tensor")),
        check_vma=False,
    )
```

profile of v0, /device:TPU:24, one launch (start us, length us, event | category | flops | bytes accessed | tf_op | source)
XLA Modules:
  0.0 901.0 jit_solution(3372570956929552600)
XLA Ops:
  7.2 0.0 copy-start
  7.2 0.0 copy-start.2
  7.2 0.0 copy-start.3
  7.2 0.0 reduce-scatter.10.cloned.1.call-start
  7.2 6.1 copy.11
  13.3 0.0 copy-done.2
  13.3 0.0 copy-done.3
  13.3 0.0 copy-start.4
  13.4 2.5 fusion.17
  15.8 0.0 copy-done.4
  15.8 2.6 fusion.16
  18.4 366.8 %all-reduce.2 = (bf16[512,1792]{1,0:T(8,128)(2,1)}, bf16[512,1792]{1,0:T(8,128)(2,1)S(1)}) all-reduce(f32[512,1792]{1,0:T(8,128)} %fusion.17, f32[512,1792]{1,0:T(8,128)} %fusion.16), channel_id=1, replica_groups=mesh['fsdp'=32,'tensor'=8] {'fsdp'}, use_global_device_ids=true, to_apply=%region_1.0 | all-reduce | flops 1835008 | bytes 11010048 | tf_op jit(solution)/shard_map/psum | solution.py:10
  385.2 0.0 copy-start.5
  385.2 0.0 copy-done
  385.3 0.0 copy-start.1
  385.3 8.2 fusion.3
  393.4 0.0 copy-done.5
  393.4 0.0 copy-done.1
  393.4 4.4 fusion.2
  397.8 0.0 copy-start.8
  397.8 1.8 copy-done.8
  399.6 2.1 fusion.8
  401.7 2.5 copy.14
  404.3 0.0 reduce-scatter.10.cloned.1.call-update
  404.3 0.0 reduce-scatter.12.cloned.1.call-start
  404.3 4.1 fusion.9
  408.4 2.4 copy.16
  410.9 0.0 reduce-scatter.12.cloned.1.call-update
  410.9 0.0 copy-start.6
  410.9 0.2 reduce-scatter.8.cloned.1.call-start
  411.2 0.0 copy-start.7
  411.2 4.9 fusion.18
  416.0 0.0 copy-done.6
  416.0 0.0 copy-done.7
  416.1 3.1 add_convert_fusion
  419.2 0.0 reduce-scatter.8.cloned.1.call-update
  419.2 199.9 %reduce-scatter.10.cloned.1.call-done = bf16[16,1792]{1,0:T(8,128)(2,1)} async-done(((bf16[512,1792]{1,0:T(8,128)(2,1)}), bf16[16,1792]{1,0:T(8,128)(2,1)}) %reduce-scatter.10.cloned.1.call-update) | async-done | bytes 57360
  619.0 1.1 copy.15
  620.1 0.8 copy.12
  621.0 222.0 %reduce-scatter.12.cloned.1.call-done = bf16[16,1792]{1,0:T(8,128)(2,1)} async-done(((bf16[512,1792]{1,0:T(8,128)(2,1)}), bf16[16,1792]{1,0:T(8,128)(2,1)}) %reduce-scatter.12.cloned.1.call-update) | async-done | bytes 57360
  843.0 1.1 copy.17
  844.1 0.8 copy.13
  844.9 49.5 %reduce-scatter.8.cloned.1.call-done = bf16[128,512]{1,0:T(8,128)(2,1)} async-done(((bf16[1024,512]{1,0:T(8,128)(2,1)}), bf16[128,512]{1,0:T(8,128)(2,1)}) %reduce-scatter.8.cloned.1.call-update) | async-done | bytes 131088 | tf_op jit(solution)/shard_map/reduce_scatter | solution.py:28
Async XLA Ops:
  7.2 378.1 %copy-start = (bf16[1024,512]{1,0:T(8,128)(2,1)S(1)}, bf16[1024,512]{1,0:T(8,128)(2,1)}, u32[]{:S(2)}) copy-start(bf16[1024,512]{1,0:T(8,128)(2,1)} %param.5) | copy-start | bytes 3145732
  7.2 6.2 copy-start.2
  7.2 6.2 copy-start.3
  7.2 611.8 %reduce-scatter.10.cloned.1.call-start = ((), (), s32[]{:S(2)}) async-start(), calls=%async_computation.4 | async-start | bytes 1892352
  13.3 2.5 copy-start.4
  385.2 8.2 copy-start.5
  385.3 8.2 copy-start.1
  397.8 1.8 copy-start.8
  404.3 438.7 %reduce-scatter.12.cloned.1.call-start = ((), (), s32[]{:S(2)}) async-start(), calls=%async_computation.5 | async-start | bytes 1892352
  410.9 5.1 copy-start.6
  410.9 483.5 %reduce-scatter.8.cloned.1.call-start = ((), (), s32[]{:S(2)}) async-start(), calls=%async_computation.3 | async-start | bytes 1179648 | tf_op jit(solution)/shard_map/reduce_scatter | solution.py:28
  411.2 4.9 copy-start.7
Sparse Core Ops, SparseCore 0:
  404.4 214.5 reduce-scatter.9
  621.7 221.2 reduce-scatter.11
  846.1 48.3 reduce-scatter.7
where the time goes:
time: 902 us; the launch traced here: 901 us
  waiting for transfers between devices  471 us (52%)
  blocking collectives  367 us (41%)
  matrix products  31.8 us (4%)
  local copies, waits for them, and re-layouts  16.8 us (2%)
  between operations  13.9 us (2%)
    unnamed x5, waiting for transfers between devices  422 us
    psum x1, blocking collectives, reduce_cores(): summed = lax.psum((gate_part, up_part), 'fsdp')  367 us
    reduce_scatter x1, waiting for transfers between devices, local(): lax.psum_scatter((total + lax.dot_general(grad_up, up_core, contract, pre...  49.5 us
  transfers between devices with their start and end apart: 3, of which 3 were waited for; matrix products, arithmetic and copies ran while one was open for 2% of the time, Pallas kernels for 0%

commit v1 on v0

v1 whole, which is shorter than its diff:
```python
import functools
import math

import jax
import jax.numpy as jnp
from jax import lax
from jax.experimental import pallas as pl
from jax.experimental.pallas import tpu as pltpu
from jax.sharding import PartitionSpec as P

BF16, F32 = jnp.bfloat16, jnp.float32
BOTH = ("fsdp", "tensor")
WIDTHS = (896, 896)
MIB = 1 << 20
SLICES = 4
K1_LIMIT = 58
SMEM = pl.BlockSpec(memory_space=pltpu.SMEM)
VMEM = pl.BlockSpec(memory_space=pltpu.VMEM)
ANY = pl.BlockSpec(memory_space=pl.ANY)
HBM = pl.BlockSpec(memory_space=pltpu.HBM)
PLACES = [(x, z, y, t) for x in range(4) for z in range(2) for y in range(4) for t in range(8)]


def index(x, z, y, t):
    return (x * 8 + z * 4 + y) * 8 + t


def along_y(t, ring):
    return (t % 2 == 0) == (ring == "a")


def shift(ring, k):
    pairs = []
    for x, z, y, t in PLACES:
        u, v = (x, (y + k) % 4) if along_y(t, ring) else ((x + k) % 4, y)
        pairs.append((index(x, z, y, t), index(u, z, v, t)))
    return pairs


SHIFTS = {ring: [shift(ring, k) for k in (1, 2, 3)] for ring in "ab"}
SWAP_Z = [(index(x, z, y, t), index(x, 1 - z, y, t)) for x, z, y, t in PLACES]
SWAP_CORE = [(t, t ^ 1) for t in range(8)]
SWAP_LOW = [[(t, t ^ 2 * bit) for t in range(8)] for bit in (1, 2)]


def send(pieces, ring):
    return [lax.ppermute(piece, BOTH, SHIFTS[ring][k]) for k, piece in enumerate(pieces)]


def swap_z(piece):
    return lax.ppermute(piece, BOTH, SWAP_Z)


def like(*shape, kind=BF16):
    return jax.ShapeDtypeStruct(shape, kind)


def call(body, out_shape, ins, after=(), limit=16, moved=MIB, name=None):
    n, skip = len(ins), len(after)

    def kernel(*refs):
        body(*refs[:n], *refs[n + skip :])

    return pl.pallas_call(
        kernel,
        out_shape=out_shape,
        in_specs=[SMEM] + [VMEM] * (n - 1) + [ANY] * skip,
        out_specs=jax.tree.map(lambda _: VMEM, out_shape),
        compiler_params=pltpu.CompilerParams(vmem_limit_bytes=limit * MIB),
        cost_estimate=pl.CostEstimate(flops=0, bytes_accessed=moved, transcendentals=0),
        name=name,
    )(*ins, *after)


def cores_body(place, basis_hbm, gate_hbm, up_hbm, own, p1, p2, p3, basis, weights, sems):
    depth = basis.shape[0]
    rows = depth // SLICES
    copies = [pltpu.make_async_copy(basis_hbm, basis, sems.at[2 * SLICES])]
    for which, source in enumerate((gate_hbm, up_hbm)):
        for i in range(SLICES):
            at = pl.ds(i * rows, rows)
            sem = sems.at[which * SLICES + i]
            copies.append(pltpu.make_async_copy(source.at[at, :], weights.at[which, at, :], sem))
    for copy in copies:
        copy.start()
    copies[0].wait()
    contract = (((0,), (0,)), ((), ()))
    for which in range(2):
        for copy in copies[1 + which * SLICES : 1 + which * SLICES + SLICES]:
            copy.wait()
        for k, ref in ((2, p2), (1, p1), (3, p3), (0, own)):
            block = lax.rem(place[0] + k, 4)
            part = basis[:, pl.ds(pl.multiple_of(block * 128, 128), 128)]
            total = lax.dot_general(part, weights[which], contract, preferred_element_type=F32)
            ref[which] = total.astype(ref.dtype)


def partial_cores(place, basis, w_gate, w_up):
    depth, width = w_gate.shape
    return pl.pallas_call(
        cores_body,
        out_shape=[like(2, 128, width)] * 4,
        in_specs=[SMEM, HBM, HBM, HBM],
        out_specs=[VMEM] * 4,
        scratch_shapes=[
            pltpu.VMEM(basis.shape, BF16),
            pltpu.VMEM((2, depth, width), BF16),
            pltpu.SemaphoreType.DMA((2 * SLICES + 1,)),
        ],
        compiler_params=pltpu.CompilerParams(vmem_limit_bytes=K1_LIMIT * MIB),
        cost_estimate=pl.CostEstimate(
            flops=4 * depth * basis.shape[1] * width, bytes_accessed=6 * MIB, transcendentals=0
        ),
        name="partial_cores",
    )(place, basis, w_gate, w_up)


def add4(own, r1, r2, r3, at):
    return (own[at].astype(F32) + r1[at].astype(F32)) + (r2[at].astype(F32) + r3[at].astype(F32))


def relay_body(place, own, r1, r2, r3, *outs):
    for k in range(4):
        rows = pl.ds(pl.multiple_of(lax.rem(place[1] + k, 4) * 32, 32), 32)
        first = 0
        for ref in outs[k::4]:
            at = (slice(None), rows, slice(first, first + ref.shape[2]))
            ref[...] = add4(own, r1, r2, r3, at).astype(ref.dtype)
            first += ref.shape[2]


def relay(place, own, pieces, widths, after=()):
    outs = []
    for cols in widths:
        outs += [like(2, 32, cols, kind=F32)] + [like(2, 32, cols)] * 3
    outs = call(relay_body, outs, (place, own, *send(pieces, "a")), after, name="relay")
    return [outs[4 * c : 4 * c + 4] for c in range(len(widths))]


def regroup_body(place, c0, c1, c2, c3, own, r1, r2, r3, *outs):
    first = c0.shape[2]
    for k, (before, ref) in enumerate(zip((c0, c1, c2, c3), outs)):
        rows = pl.ds(pl.multiple_of(lax.rem(place[1] + k, 4) * 32, 32), 32)
        value = add4(own, r1, r2, r3, (slice(None), rows, slice(None)))
        ref[:, :, :first] = before[...]
        ref[:, :, first:] = value.astype(ref.dtype)


def sum4_body(place, own, r1, r2, r3, out):
    out[...] = add4(own, r1, r2, r3, ...).astype(out.dtype)


def add2_body(place, a, b, out):
    out[...] = (a[...].astype(F32) + b[...].astype(F32)).astype(BF16)


def join_body(place, *refs):
    outs = refs[len(refs) // 5 * 4 :]
    for chunk, out in enumerate(outs):
        for k, ref in enumerate(refs[4 * chunk : 4 * chunk + 4]):
            at = pl.ds(pl.multiple_of(lax.rem(place[1] + 4 - k, 4) * 32, 32), 32)
            out[:, at, :] = ref[...]


def main_body(scale, start, place, coeffs, c0, c1, c2, c3, hidden_hbm, *rest):
    first = start == 0
    if first:
        dcoeffs, own, p1, p2, p3, core, grads, hidden, sems = rest
    else:
        before, kept, sent, own, p1, p2, p3, core, grads, hidden, sems = rest
    step, steps = pl.program_id(0), pl.num_programs(0)
    tile = coeffs.shape[0]

    def fetch(i):
        rows = pl.ds(pl.multiple_of(i * tile, tile), tile)
        source = hidden_hbm.at[rows, pl.ds(start, hidden.shape[2])]
        return pltpu.make_async_copy(source, hidden.at[i], sems.at[i])

    @pl.when(step == 0)
    def _():
        for i in range(hidden.shape[0]):
            fetch(i).start()
        for k, ref in enumerate((c0, c1, c2, c3)):
            at = pl.multiple_of(lax.rem(place[0] + 4 - k, 4) * 128, 128)
            core[:, pl.ds(at, 128), :] = ref[...]

    x = coeffs[...]
    gate = jnp.dot(x, core[0], preferred_element_type=F32)
    upward = jnp.dot(x, core[1], preferred_element_type=F32)
    sig = 0.5 * jnp.tanh(0.5 * gate) + 0.5
    fetch(step).wait()
    scaled = hidden[step].astype(F32) * sig
    grad_gate = (scaled * upward * (1.0 + gate * (1.0 - sig))).astype(BF16)
    grad_up = (scaled * gate).astype(BF16)
    contract = (((1,), (1,)), ((), ()))
    total = lax.dot_general(grad_gate, core[0], contract, preferred_element_type=F32)
    total += lax.dot_general(grad_up, core[1], contract, preferred_element_type=F32)
    if first:
        dcoeffs[...] = total
    else:
        total += before[...]
        for half in range(2):
            rows = total[128 * half : 128 * half + 128]

            @pl.when(place[5] == half)
            def _():
                kept[...] = rows

            @pl.when(place[5] != half)
            def _():
                sent[...] = rows.astype(BF16)

    contract = (((0,), (0,)), ((), ()))
    gate_term = lax.dot_general(x, grad_gate, contract, preferred_element_type=F32)
    up_term = lax.dot_general(x, grad_up, contract, preferred_element_type=F32)

    @pl.when(step == 0)
    def _():
        grads[0], grads[1] = gate_term, up_term

    @pl.when(step > 0)
    def _():
        grads[0] += gate_term
        grads[1] += up_term

    @pl.when(step == steps - 1)
    def _():
        for k, ref in enumerate((own, p1, p2, p3)):
            block = lax.rem(place[0] + k, 4)
            for s in range(8):
                row = block * place[2] + (s // 2) * place[3] + (s % 2) * 64
                for which in range(2):
                    value = grads[which, pl.ds(pl.multiple_of(row, 16), 16), :] * scale
                    ref[which, s * 16 : s * 16 + 16, :] = value.astype(ref.dtype)


def main(place, coeffs, cores, hidden, before, start, cols, scale):
    tokens, rank = coeffs.shape
    tile = 256
    first = before is None
    whole = pl.BlockSpec((2, 128, cols), lambda i: (0, 0, 0))
    row_block = pl.BlockSpec((tile, rank), lambda i: (i, 0))
    half_block = pl.BlockSpec((tile // 2, rank), lambda i: (i, 0))
    if first:
        outs, specs = [like(tokens, rank, kind=F32)], [row_block]
    else:
        outs = [like(tokens // 2, rank, kind=F32), like(tokens // 2, rank)]
        specs = [half_block] * 2
    return pl.pallas_call(
        functools.partial(main_body, scale, start),
        grid=(tokens // tile,),
        out_shape=outs + [like(2, 128, cols, kind=F32)] + [like(2, 128, cols)] * 3,
        in_specs=[SMEM, row_block]
        + [whole] * 4
        + [HBM]
        + ([] if first else [row_block]),
        out_specs=specs + [whole] * 4,
        scratch_shapes=[
            pltpu.VMEM((2, rank, cols), BF16),
            pltpu.VMEM((2, rank, cols), F32),
            pltpu.VMEM((tokens // tile, tile, cols), BF16),
            pltpu.SemaphoreType.DMA((tokens // tile,)),
        ],
        compiler_params=pltpu.CompilerParams(vmem_limit_bytes=32 * MIB),
        cost_estimate=pl.CostEstimate(
            flops=12 * tokens * rank * cols,
            bytes_accessed=10 * MIB,
            transcendentals=tokens * cols,
        ),
        name="main",
    )(place, coeffs, *cores, hidden, *([] if first else [before]))


def halve_body(place, own, r1, r2, r3, kept, sent):
    for ref, half in ((kept, place[4]), (sent, 1 - place[4])):
        at = (slice(None), pl.ds(pl.multiple_of(half * 16, 16), 16), slice(None))
        ref[...] = add4(own, r1, r2, r3, at).astype(ref.dtype)


def last_body(place, own, got, *refs):
    tokens, gate, up = refs[-3:]
    tokens[...] = (own[...] + got[...].astype(F32)).astype(BF16)
    first = 0
    for kept, got in zip(refs[:-3:2], refs[1:-3:2]):
        cols = slice(first, first + kept.shape[2])
        gate[:, cols] = kept[0] + got[0].astype(F32)
        up[:, cols] = kept[1] + got[1].astype(F32)
        first += kept.shape[2]


def tokens_body(place, total, got, kept, sent):
    for ref, flip in ((kept, 0), (sent, 1)):
        for i in range(2):
            block = place[6] ^ (flip + 2 * i)
            at = (pl.ds(pl.multiple_of(block * 128, 128), 128), slice(None))
            value = total[at] + got[at].astype(F32)
            ref[128 * i : 128 * i + 128, :] = value.astype(ref.dtype)


def tokens_half_body(place, total, got, kept, sent):
    kept[...] = total[:128] + got[:128].astype(F32)
    sent[...] = (total[128:] + got[128:].astype(F32)).astype(BF16)


def scatter_tokens(place, kept, sent):
    rank = kept.shape[1]
    got = lax.ppermute(sent, "tensor", SWAP_CORE)
    for size, body, name in ((256, tokens_body, "tokens"), (128, tokens_half_body, "tokens_half")):
        outs = [like(size, rank, kind=F32), like(size, rank)]
        kept, sent = call(body, outs, (place, kept, got), name=name)
        got = lax.ppermute(sent, "tensor", SWAP_LOW[size == 128])
    return [kept, got]


def local(coeffs, pca_basis, w_gate, w_up, grad_hidden):
    fsdp, tensor = lax.axis_index("fsdp"), lax.axis_index("tensor")
    core, low = tensor & 1, tensor >> 1
    x, z, y = fsdp >> 3, (fsdp >> 2) & 1, fsdp & 3
    a, b = jnp.where(core == 0, y, x), jnp.where(core == 0, x, y)
    stride_a, stride_b = jnp.where(core == 0, 16, 128), jnp.where(core == 0, 128, 16)
    place = jnp.stack([a, b, stride_a, stride_b, z, core, low]).astype(jnp.int32)
    width = w_gate.shape[1]
    scale = 1.0 / math.sqrt(coeffs.shape[0] * 32)
    starts = [sum(WIDTHS[:c]) for c in range(len(WIDTHS))]

    own, *pieces = partial_cores(place, pca_basis, w_gate, w_up)
    halves, cores = [], []
    for cols, (own, *pieces) in zip(WIDTHS, relay(place, own, pieces, WIDTHS)):
        ins = (place, own, *send(pieces, "b"))
        halves.append(call(sum4_body, like(2, 32, cols), ins, name="sum4"))
    for cols, half in zip(WIDTHS, halves):
        ins = (place, half, swap_z(half))
        cores.append(call(add2_body, like(2, 32, cols), ins, halves[-1:], name="add2"))
    ins = [place]
    for core in cores:
        ins += [core] + send([core] * 3, "b")
    blocks = call(join_body, [like(2, 128, cols) for cols in WIDTHS], ins, name="join")
    cores = [[block] + send([block] * 3, "a") for block in blocks]
    total, grads = [None], []
    for start, cols, core in zip(starts, WIDTHS, cores):
        *total, own, p1, p2, p3 = main(
            place, coeffs, core, grad_hidden, total[0], start, cols, scale
        )
        grads.append((own, p1, p2, p3))
    own, *pieces = grads[0]
    parts = list(relay(place, own, pieces, WIDTHS[:1], total[:1])[0])
    tokens = scatter_tokens(place, *total)
    own, *pieces = grads[1]
    parts += [own] + send(pieces, "a")
    outs = [like(2, 32, width, kind=F32)] + [like(2, 32, width)] * 3
    own, *pieces = call(regroup_body, outs, (place, *parts), tokens[:1], name="regroup")
    outs = [like(2, 16, width, kind=F32), like(2, 16, width)]
    kept, sent = call(halve_body, outs, (place, own, *send(pieces, "b")), name="halve")
    ends = [kept, swap_z(sent)]
    outs = [like(*tokens[0].shape), like(16, width, kind=F32), like(16, width, kind=F32)]
    return call(last_body, outs, (place, *tokens, *ends), name="last")


def solution(mesh):
    placed = (
        P("fsdp", None),
        P("fsdp", None),
        P("fsdp", "tensor"),
        P("fsdp", "tensor"),
        P("fsdp", "tensor"),
    )
    return jax.shard_map(
        local,
        mesh=mesh,
        in_specs=placed,
        out_specs=(P(BOTH, None), P("fsdp", "tensor"), P("fsdp", "tensor")),
        check_vma=False,
    )
```

time: 902 us -> 170 us (0.19)
  waiting for transfers between devices: 471 us -> 56.8 us
  blocking collectives: 367 us -> 0 us
  starting transfers between devices: 0.3 us -> 73.2 us
  Pallas kernels: 0 us -> 36 us
  matrix products: 31.8 us -> 0 us
  local copies, waits for them, and re-layouts: 16.8 us -> 2.42 us
  between operations: 13.9 us -> 0.86 us
    unnamed x5 -> x0, waiting for transfers between devices: 422 us -> none
    psum x1 -> x0, blocking collectives: 367 us -> none  [reduce_cores(): summed = lax.psum((gate_part, up_part), 'fsdp')]
    ppermute x0 -> x36, starting transfers between devices: none -> 73.2 us  [the longest x30 41 us: send(): lax.ppermute(piece, BOTH, SHIFTS[ring][k])]
    ppermute x0 -> x36, waiting for transfers between devices: none -> 56.8 us  [the longest x30 49.1 us: send(): lax.ppermute(piece, BOTH, SHIFTS[ring][k])]
    reduce_scatter x1 -> x0, waiting for transfers between devices: 49.5 us -> none  [local(): lax.psum_scatter((total + lax.dot_general(grad_up, up_core, contract, pre...]
    pallas_call x0 -> x15, Pallas kernels: none -> 36 us  [the longest x2 22.3 us: main(): pl.pallas_call(functools.partial(main_body, scale, start), grid=(tokens /...]
    dot_general x8 -> x0, matrix products: 31.8 us -> none  [the longest x1 8.15 us: local(): gate = jnp.dot(coeffs, gate_core, preferred_element_type=jnp.float32)]
    unnamed x25 -> x10, local copies, waits for them, and re-layouts: 16.8 us -> 1.8 us
  transfers between devices with their start and end apart: 3 -> 36, of which waited for: 3 -> 15; matrix products, arithmetic and copies ran while one was open for 2% -> 0% of each run, Pallas kernels for 0% -> 9%
where the time goes in v1:
time: 170 us; the launch traced here: 169 us
  starting transfers between devices  73.2 us (43%)
  waiting for transfers between devices  56.8 us (33%)
  Pallas kernels  36 us (21%)
  local copies, waits for them, and re-layouts  2.42 us (1%)
    ppermute x30, waiting for transfers between devices, send(): lax.ppermute(piece, BOTH, SHIFTS[ring][k])  49.1 us
    ppermute x30, starting transfers between devices, send(): lax.ppermute(piece, BOTH, SHIFTS[ring][k])  41 us
    pallas_call x2, Pallas kernels, main(): pl.pallas_call(functools.partial(main_body, scale, start), grid=(tokens /...  22.3 us
    ppermute x3, starting transfers between devices, swap_z(): return lax.ppermute(piece, BOTH, SWAP_Z)  21.8 us
    ppermute x2, starting transfers between devices, scatter_tokens(): got = lax.ppermute(sent, 'tensor', SWAP_LOW[size == 128])  10.1 us
    pallas_call x12, Pallas kernels, call(): pl.pallas_call(kernel, out_shape=out_shape, in_specs=[SMEM] + [VMEM] * (n...  8.63 us
    pallas_call x1, Pallas kernels, partial_cores(): pl.pallas_call(cores_body, out_shape=[like(2, 128, width)] * 4, in_specs=...  5.12 us
    ppermute x3, waiting for transfers between devices, swap_z(): return lax.ppermute(piece, BOTH, SWAP_Z)  4.2 us
  transfers between devices with their start and end apart: 36, of which 15 were waited for; matrix products, arithmetic and copies ran while one was open for 0% of the time, Pallas kernels for 9%

profile of v1, /device:TPU:24, one launch (start us, length us, event | category | flops | bytes accessed | tf_op | source)
XLA Modules:
  0.0 169.4 jit_solution(2931839767200054177)
XLA Ops:
  0.6 0.6 stack.31.place.refs_0_
  1.3 5.1 %partial_cores.1 = (bf16[2,128,1792]{2,1,0:T(8,128)(2,1)}, bf16[2,128,1792]{2,1,0:T(8,128)(2,1)}, bf16[2,128,1792]{2,1,0:T(8,128)(2,1)}, bf16[2,128,1792]{2,1,0:T(8,128)(2,1)}) custom-call(s32[7]{0:T(128)} %stack.31.place.refs_0_, bf16[256,512]{1,0:T(8,128)(2,1)} %basis_hbm.1, bf16[256,1792]{1,0:T(8,128)(2,1)} %gate_hbm.1, bf16[256,1792]{1,0:T(8,128)(2,1)} %up_hbm.1), custom_call_target="tpu_custom_call" | custom-call | flops 939524096 | bytes 6291456 | tf_op jit(solution)/shard_map/partial_cores/pallas_call | solution.py:100
  6.4 2.0 %collective-permute-start = (bf16[2,128,1792]{2,1,0:T(8,128)(2,1)}, bf16[2,128,1792]{2,1,0:T(8,128)(2,1)S(1)}, u32[]{:S(2)}, u32[]{:S(2)}) collective-permute-start(bf16[2,128,1792]{2,1,0:T(8,128)(2,1)} %get-tuple-element.43), channel_id=1, source_target_pairs={{0,8},{1,65},{2,10},{3,67},{4,12},{5,69},{6,14},{7,71},{8,16},{9,7... | collective-permute-start | bytes 2752520 | tf_op jit(solution)/shard_map/ppermute | solution.py:47
  8.4 0.8 collective-permute-start.1
  9.4 20.1 %collective-permute-done.refs_2_ = bf16[2,128,1792]{2,1,0:T(8,128)(2,1)S(1)} collective-permute-done((bf16[2,128,1792]{2,1,0:T(8,128)(2,1)}, bf16[2,128,1792]{2,1,0:T(8,128)(2,1)S(1)}, u32[]{:S(2)}, u32[]{:S(2)}) %collective-permute-start) | collective-permute-done | bytes 917536 | tf_op jit(solution)/shard_map/ppermute | solution.py:47
  29.5 3.8 %collective-permute-done.2.refs_4_ = bf16[2,128,1792]{2,1,0:T(8,128)(2,1)S(1)} collective-permute-done((bf16[2,128,1792]{2,1,0:T(8,128)(2,1)}, bf16[2,128,1792]{2,1,0:T(8,128)(2,1)S(1)}, u32[]{:S(2)}, u32[]{:S(2)}) %collective-permute-start.2) | collective-permute-done | bytes 917536 | tf_op jit(solution)/shard_map/ppermute | solution.py:47
  33.4 1.2 copy-done
  35.2 1.0 relay.2
  36.2 2.5 %collective-permute-start.4 = (bf16[2,32,896]{2,1,0:T(8,128)(2,1)S(1)}, bf16[2,32,896]{2,1,0:T(8,128)(2,1)S(1)}, u32[]{:S(2)}, u32[]{:S(2)}) collective-permute-start(bf16[2,32,896]{2,1,0:T(8,128)(2,1)S(1)} %get-tuple-element.48), channel_id=1, source_target_pairs={{0,128},{1,17},{2,130},{3,19},{4,132},{5,21},{6,134},{7,23},{8,136... | collective-permute-start | bytes 344072 | tf_op jit(solution)/shard_map/ppermute | solution.py:47
  38.7 1.4 collective-permute-start.5
  40.7 1.7 collective-permute-start.8
  42.4 1.1 collective-permute-done.3.refs_2_
  43.5 1.6 collective-permute-start.9
  45.6 5.7 %collective-permute-start.6 = (bf16[2,32,896]{2,1,0:T(8,128)(2,1)S(1)}, bf16[2,32,896]{2,1,0:T(8,128)(2,1)S(1)}, u32[]{:S(2)}, u32[]{:S(2)}) collective-permute-start(bf16[2,32,896]{2,1,0:T(8,128)(2,1)S(1)} %sum4.2.refs_1_), channel_id=1, source_target_pairs={{0,32},{1,33},{2,34},{3,35},{4,36},{5,37},{6,38},{7,39},{8,40},{9,... | collective-permute-start | bytes 344072 | tf_op jit(solution)/shard_map/ppermute | solution.py:51
  52.0 4.2 %collective-permute-start.13 = (bf16[2,32,896]{2,1,0:T(8,128)(2,1)S(1)}, bf16[2,32,896]{2,1,0:T(8,128)(2,1)S(1)}, u32[]{:S(2)}, u32[]{:S(2)}) collective-permute-start(bf16[2,32,896]{2,1,0:T(8,128)(2,1)S(1)} %sum4.3.refs_3_.refs_1_), channel_id=1, source_target_pairs={{0,32},{1,33},{2,34},{3,35},{4,36},{5,37},{6,38},{7,39},{8,40},{9,... | collective-permute-start | bytes 344072 | tf_op jit(solution)/shard_map/ppermute | solution.py:51
  56.7 2.7 %collective-permute-start.12 = (bf16[2,32,896]{2,1,0:T(8,128)(2,1)S(1)}, bf16[2,32,896]{2,1,0:T(8,128)(2,1)S(1)}, u32[]{:S(2)}, u32[]{:S(2)}) collective-permute-start(bf16[2,32,896]{2,1,0:T(8,128)(2,1)S(1)} %add2.2.refs_1_), channel_id=1, source_target_pairs={{0,192},{1,25},{2,194},{3,27},{4,196},{5,29},{6,198},{7,31},{8,200... | collective-permute-start | bytes 344072 | tf_op jit(solution)/shard_map/ppermute | solution.py:47
  59.7 1.3 collective-permute-start.10
  61.8 3.0 %collective-permute-start.16 = (bf16[2,32,896]{2,1,0:T(8,128)(2,1)S(1)}, bf16[2,32,896]{2,1,0:T(8,128)(2,1)S(1)}, u32[]{:S(2)}, u32[]{:S(2)}) collective-permute-start(bf16[2,32,896]{2,1,0:T(8,128)(2,1)S(1)} %add2.3.refs_5_), channel_id=1, source_target_pairs={{0,192},{1,25},{2,194},{3,27},{4,196},{5,29},{6,198},{7,31},{8,200... | collective-permute-start | bytes 344072 | tf_op jit(solution)/shard_map/ppermute | solution.py:47
  64.9 1.1 collective-permute-start.15
  66.0 0.9 collective-permute-start.14
  67.2 4.0 %collective-permute-done.15.refs_7_ = bf16[2,32,896]{2,1,0:T(8,128)(2,1)S(1)} collective-permute-done((bf16[2,32,896]{2,1,0:T(8,128)(2,1)S(1)}, bf16[2,32,896]{2,1,0:T(8,128)(2,1)S(1)}, u32[]{:S(2)}, u32[]{:S(2)}) %collective-permute-start.15) | collective-permute-done | bytes 114720 | tf_op jit(solution)/shard_map/ppermute | solution.py:47
  71.2 1.5 collective-permute-done.14.refs_6_
  72.7 0.6 join.1
  73.8 1.8 %collective-permute-start.21 = (bf16[2,128,896]{2,1,0:T(8,128)(2,1)S(1)}, bf16[2,128,896]{2,1,0:T(8,128)(2,1)S(1)}, u32[]{:S(2)}, u32[]{:S(2)}) collective-permute-start(bf16[2,128,896]{2,1,0:T(8,128)(2,1)S(1)} %get-tuple-element.55.c0), channel_id=1, source_target_pairs={{0,16},{1,129},{2,18},{3,131},{4,20},{5,133},{6,22},{7,135},{8,24}... | collective-permute-start | bytes 1376264 | tf_op jit(solution)/shard_map/ppermute | solution.py:47
  75.5 1.8 %collective-permute-start.20 = (bf16[2,128,896]{2,1,0:T(8,128)(2,1)S(1)}, bf16[2,128,896]{2,1,0:T(8,128)(2,1)S(1)}, u32[]{:S(2)}, u32[]{:S(2)}) collective-permute-start(bf16[2,128,896]{2,1,0:T(8,128)(2,1)S(1)} %get-tuple-element.55.c0), channel_id=1, source_target_pairs={{0,8},{1,65},{2,10},{3,67},{4,12},{5,69},{6,14},{7,71},{8,16},{9,7... | collective-permute-start | bytes 1376264 | tf_op jit(solution)/shard_map/ppermute | solution.py:47
  77.5 2.0 %collective-permute-start.18 = (bf16[2,128,896]{2,1,0:T(8,128)(2,1)S(1)}, bf16[2,128,896]{2,1,0:T(8,128)(2,1)S(1)}, u32[]{:S(2)}, u32[]{:S(2)}) collective-permute-start(bf16[2,128,896]{2,1,0:T(8,128)(2,1)S(1)} %get-tuple-element.54.c0), channel_id=1, source_target_pairs={{0,16},{1,129},{2,18},{3,131},{4,20},{5,133},{6,22},{7,135},{8,24}... | collective-permute-start | bytes 1376264 | tf_op jit(solution)/shard_map/ppermute | solution.py:47
  79.5 8.4 %collective-permute-done.22.c3 = bf16[2,128,896]{2,1,0:T(8,128)(2,1)S(1)} collective-permute-done((bf16[2,128,896]{2,1,0:T(8,128)(2,1)S(1)}, bf16[2,128,896]{2,1,0:T(8,128)(2,1)S(1)}, u32[]{:S(2)}, u32[]{:S(2)}) %collective-permute-start.22) | collective-permute-done | bytes 458784 | tf_op jit(solution)/shard_map/ppermute | solution.py:47
  88.0 0.9 collective-permute-done.20.c1
  88.9 10.7 %main.2 = (f32[1024,512]{1,0:T(8,128)S(1)}, f32[2,128,896]{2,1,0:T(8,128)S(1)}, bf16[2,128,896]{2,1,0:T(8,128)(2,1)S(1)}, bf16[2,128,896]{2,1,0:T(8,128)(2,1)S(1)}, bf16[2,128,896]{2,1,0:T(8,128)(2,1)S(1)}) custom-call(s32[7]{0:T(128)S(1)} %copy-done.2, bf16[1024,512]{1,0:T(8,128)(2,1)S(1)} %copy-done.4, bf16[2,128,896]{2,1,0:T(8,128)(2,1)S(1)} %get-tuple-element.55.c0, ...), custom_call_target="tpu_custom_call" | custom-call | flops 5637144576 | bytes 10485760 | tf_op jit(solution)/shard_map/main/pallas_call | solution.py:249
  99.6 11.6 %main.3 = (f32[512,512]{1,0:T(8,128)S(1)}, bf16[512,512]{1,0:T(8,128)(2,1)S(1)}, f32[2,128,896]{2,1,0:T(8,128)S(1)}, bf16[2,128,896]{2,1,0:T(8,128)(2,1)S(1)}, b...) custom-call(s32[7]{0:T(128)S(1)} %copy-done.2, bf16[1024,512]{1,0:T(8,128)(2,1)S(1)} %copy-done.4, ...), custom_call_target="tpu_custom_call" | custom-call | flops 5637144576 | bytes 10485760 | tf_op jit(solution)/shard_map/main/pallas_call | solution.py:249
  111.5 2.7 %collective-permute-start.26 = (bf16[2,128,896]{2,1,0:T(8,128)(2,1)S(1)}, bf16[2,128,896]{2,1,0:T(8,128)(2,1)S(1)}, u32[]{:S(2)}, u32[]{:S(2)}) collective-permute-start(bf16[2,128,896]{2,1,0:T(8,128)(2,1)S(1)} %get-tuple-element.64), channel_id=1, source_target_pairs={{0,8},{1,65},{2,10},{3,67},{4,12},{5,69},{6,14},{7,71},{8,16},{9,7... | collective-permute-start | bytes 1376264 | tf_op jit(solution)/shard_map/ppermute | solution.py:47
  115.2 2.9 %collective-permute-start.29 = (bf16[2,128,896]{2,1,0:T(8,128)(2,1)S(1)}, bf16[2,128,896]{2,1,0:T(8,128)(2,1)S(1)}, u32[]{:S(2)}, u32[]{:S(2)}) collective-permute-start(bf16[2,128,896]{2,1,0:T(8,128)(2,1)S(1)} %get-tuple-element.72), channel_id=1, source_target_pairs={{0,8},{1,65},{2,10},{3,67},{4,12},{5,69},{6,14},{7,71},{8,16},{9,7... | collective-permute-start | bytes 1376264 | tf_op jit(solution)/shard_map/ppermute | solution.py:47
  118.1 7.1 %collective-permute-done.26.refs_2_ = bf16[2,128,896]{2,1,0:T(8,128)(2,1)S(1)} collective-permute-done((bf16[2,128,896]{2,1,0:T(8,128)(2,1)S(1)}, bf16[2,128,896]{2,1,0:T(8,128)(2,1)S(1)}, u32[]{:S(2)}, u32[]{:S(2)}) %collective-permute-start.26) | collective-permute-done | bytes 458784 | tf_op jit(solution)/shard_map/ppermute | solution.py:47
  125.2 4.5 %collective-permute-start.31 = (bf16[2,128,896]{2,1,0:T(8,128)(2,1)S(1)}, bf16[2,128,896]{2,1,0:T(8,128)(2,1)S(1)}, u32[]{:S(2)}, u32[]{:S(2)}) collective-permute-start(bf16[2,128,896]{2,1,0:T(8,128)(2,1)S(1)} %get-tuple-element.74), channel_id=1, source_target_pairs={{0,24},{1,193},{2,26},{3,195},{4,28},{5,197},{6,30},{7,199},{8,0},... | collective-permute-start | bytes 1376264 | tf_op jit(solution)/shard_map/ppermute | solution.py:47
  129.7 0.6 tokens.1
  130.4 4.6 %collective-permute-start.24 = (bf16[256,512]{1,0:T(8,128)(2,1)S(1)}, bf16[256,512]{1,0:T(8,128)(2,1)S(1)}, u32[]{:S(2)}, u32[]{:S(2)}) collective-permute-start(bf16[256,512]{1,0:T(8,128)(2,1)S(1)} %get-tuple-element.60), channel_id=1, source_target_pairs={{0,2},{1,3},{2,0},{3,1},{4,6},{5,7},{6,4},{7,5},{8,10},{9,11},{10,... | collective-permute-start | bytes 786440 | tf_op jit(solution)/shard_map/ppermute | solution.py:311
  134.9 0.8 relay.3
  135.7 3.6 %collective-permute-done.24.refs_2_ = bf16[256,512]{1,0:T(8,128)(2,1)S(1)} collective-permute-done((bf16[256,512]{1,0:T(8,128)(2,1)S(1)}, bf16[256,512]{1,0:T(8,128)(2,1)S(1)}, u32[]{:S(2)}, u32[]{:S(2)}) %collective-permute-start.24) | collective-permute-done | bytes 262176 | tf_op jit(solution)/shard_map/ppermute | solution.py:311
  140.1 0.8 regroup.1
  140.9 2.3 %collective-permute-start.33 = (bf16[2,32,1792]{2,1,0:T(8,128)(2,1)S(1)}, bf16[2,32,1792]{2,1,0:T(8,128)(2,1)S(1)}, u32[]{:S(2)}, u32[]{:S(2)}) collective-permute-start(bf16[2,32,1792]{2,1,0:T(8,128)(2,1)S(1)} %get-tuple-element.77), channel_id=1, source_target_pairs={{0,128},{1,17},{2,130},{3,19},{4,132},{5,21},{6,134},{7,23},{8,136... | collective-permute-start | bytes 688136 | tf_op jit(solution)/shard_map/ppermute | solution.py:47
  143.3 1.2 collective-permute-start.34
  144.4 5.5 %collective-permute-start.25 = (bf16[128,512]{1,0:T(8,128)(2,1)S(1)}, bf16[128,512]{1,0:T(8,128)(2,1)S(1)}, u32[]{:S(2)}, u32[]{:S(2)}) collective-permute-start(bf16[128,512]{1,0:T(8,128)(2,1)S(1)} %get-tuple-element.62), channel_id=1, source_target_pairs={{0,4},{1,5},{2,6},{3,7},{4,0},{5,1},{6,2},{7,3},{8,12},{9,13},{10,... | collective-permute-start | bytes 393224 | tf_op jit(solution)/shard_map/ppermute | solution.py:311
  149.9 0.7 collective-permute-done.32.refs_2_
  150.6 0.9 collective-permute-done.34.refs_4_
  151.5 0.7 halve.1
  152.2 11.9 %collective-permute-start.35 = (bf16[2,16,1792]{2,1,0:T(8,128)(2,1)S(1)}, bf16[2,16,1792]{2,1,0:T(8,128)(2,1)S(1)}, u32[]{:S(2)}, u32[]{:S(2)}) collective-permute-start(bf16[2,16,1792]{2,1,0:T(8,128)(2,1)S(1)} %get-tuple-element.80), channel_id=1, source_target_pairs={{0,32},{1,33},{2,34},{3,35},{4,36},{5,37},{6,38},{7,39},{8,40},{9,... | collective-permute-start | bytes 344072 | tf_op jit(solution)/shard_map/ppermute | solution.py:51
  164.1 3.9 %collective-permute-done.35.refs_4_ = bf16[2,16,1792]{2,1,0:T(8,128)(2,1)S(1)} collective-permute-done((bf16[2,16,1792]{2,1,0:T(8,128)(2,1)S(1)}, bf16[2,16,1792]{2,1,0:T(8,128)(2,1)S(1)}, u32[]{:S(2)}, u32[]{:S(2)}) %collective-permute-start.35) | collective-permute-done | bytes 114720 | tf_op jit(solution)/shard_map/ppermute | solution.py:51
  168.1 1.3 last.1
  (50 shorter events, 7.5 us)
Async XLA Ops:
  1.3 87.6 %copy-start.4 = (bf16[1024,512]{1,0:T(8,128)(2,1)S(1)}, bf16[1024,512]{1,0:T(8,128)(2,1)}, u32[]{:S(2)}) copy-start(bf16[1024,512]{1,0:T(8,128)(2,1)} %coeffs.3) | copy-start | bytes 3145732
  6.4 82.5 %copy-start.2 = (s32[7]{0:T(128)S(1)}, s32[7]{0:T(128)}, u32[]{:S(2)}) copy-start(s32[7]{0:T(128)} %stack.31.place.refs_0_) | copy-start | bytes 88
  6.4 23.1 %collective-permute-start = (bf16[2,128,1792]{2,1,0:T(8,128)(2,1)}, bf16[2,128,1792]{2,1,0:T(8,128)(2,1)S(1)}, u32[]{:S(2)}, u32[]{:S(2)}) collective-permute-start(bf16[2,128,1792]{2,1,0:T(8,128)(2,1)} %get-tuple-element.43), channel_id=1, source_target_pairs={{0,8},{1,65},{2,10},{3,67},{4,12},{5,69},{6,14},{7,71},{8,16},{9,7... | collective-permute-start | bytes 2752520 | tf_op jit(solution)/shard_map/ppermute | solution.py:47
  8.4 21.1 %collective-permute-start.1 = (bf16[2,128,1792]{2,1,0:T(8,128)(2,1)}, bf16[2,128,1792]{2,1,0:T(8,128)(2,1)S(1)}, u32[]{:S(2)}, u32[]{:S(2)}) collective-permute-start(bf16[2,128,1792]{2,1,0:T(8,128)(2,1)} %get-tuple-element.44), channel_id=1, source_target_pairs={{0,16},{1,129},{2,18},{3,131},{4,20},{5,133},{6,22},{7,135},{8,24}... | collective-permute-start | bytes 2752520 | tf_op jit(solution)/shard_map/ppermute | solution.py:47
  9.3 24.1 %collective-permute-start.2 = (bf16[2,128,1792]{2,1,0:T(8,128)(2,1)}, bf16[2,128,1792]{2,1,0:T(8,128)(2,1)S(1)}, u32[]{:S(2)}, u32[]{:S(2)}) collective-permute-start(bf16[2,128,1792]{2,1,0:T(8,128)(2,1)} %get-tuple-element.45), channel_id=1, source_target_pairs={{0,24},{1,193},{2,26},{3,195},{4,28},{5,197},{6,30},{7,199},{8,0},... | collective-permute-start | bytes 2752520 | tf_op jit(solution)/shard_map/ppermute | solution.py:47
  33.4 1.2 copy-start
  34.5 0.6 copy-start.1
  35.2 53.7 %copy-start.3 = (bf16[1024,1792]{1,0:T(8,128)(2,1)S(1)}, bf16[1024,1792]{1,0:T(8,128)(2,1)}, u32[]{:S(2)}) copy-start(bf16[1024,1792]{1,0:T(8,128)(2,1)} %hidden_hbm.3) | copy-start | bytes 11010052
  36.2 7.3 %collective-permute-start.3 = (bf16[2,32,896]{2,1,0:T(8,128)(2,1)S(1)}, bf16[2,32,896]{2,1,0:T(8,128)(2,1)S(1)}, u32[]{:S(2)}, u32[]{:S(2)}) collective-permute-start(bf16[2,32,896]{2,1,0:T(8,128)(2,1)S(1)} %get-tuple-element.47), channel_id=1, source_target_pairs={{0,64},{1,9},{2,66},{3,11},{4,68},{5,13},{6,70},{7,15},{8,72},{9,1... | collective-permute-start | bytes 344072 | tf_op jit(solution)/shard_map/ppermute | solution.py:47
  36.2 8.8 %collective-permute-start.4 = (bf16[2,32,896]{2,1,0:T(8,128)(2,1)S(1)}, bf16[2,32,896]{2,1,0:T(8,128)(2,1)S(1)}, u32[]{:S(2)}, u32[]{:S(2)}) collective-permute-start(bf16[2,32,896]{2,1,0:T(8,128)(2,1)S(1)} %get-tuple-element.48), channel_id=1, source_target_pairs={{0,128},{1,17},{2,130},{3,19},{4,132},{5,21},{6,134},{7,23},{8,136... | collective-permute-start | bytes 344072 | tf_op jit(solution)/shard_map/ppermute | solution.py:47
  38.7 6.3 %collective-permute-start.5 = (bf16[2,32,896]{2,1,0:T(8,128)(2,1)S(1)}, bf16[2,32,896]{2,1,0:T(8,128)(2,1)S(1)}, u32[]{:S(2)}, u32[]{:S(2)}) collective-permute-start(bf16[2,32,896]{2,1,0:T(8,128)(2,1)S(1)} %get-tuple-element.49), channel_id=1, source_target_pairs={{0,192},{1,25},{2,194},{3,27},{4,196},{5,29},{6,198},{7,31},{8,200... | collective-permute-start | bytes 344072 | tf_op jit(solution)/shard_map/ppermute | solution.py:47
  40.1 11.3 %collective-permute-start.7 = (bf16[2,32,896]{2,1,0:T(8,128)(2,1)S(1)}, bf16[2,32,896]{2,1,0:T(8,128)(2,1)S(1)}, u32[]{:S(2)}, u32[]{:S(2)}) collective-permute-start(bf16[2,32,896]{2,1,0:T(8,128)(2,1)S(1)} %get-tuple-element.51), channel_id=1, source_target_pairs={{0,64},{1,9},{2,66},{3,11},{4,68},{5,13},{6,70},{7,15},{8,72},{9,1... | collective-permute-start | bytes 344072 | tf_op jit(solution)/shard_map/ppermute | solution.py:47
  40.7 10.7 %collective-permute-start.8 = (bf16[2,32,896]{2,1,0:T(8,128)(2,1)S(1)}, bf16[2,32,896]{2,1,0:T(8,128)(2,1)S(1)}, u32[]{:S(2)}, u32[]{:S(2)}) collective-permute-start(bf16[2,32,896]{2,1,0:T(8,128)(2,1)S(1)} %get-tuple-element.52), channel_id=1, source_target_pairs={{0,128},{1,17},{2,130},{3,19},{4,132},{5,21},{6,134},{7,23},{8,136... | collective-permute-start | bytes 344072 | tf_op jit(solution)/shard_map/ppermute | solution.py:47
  43.5 7.9 %collective-permute-start.9 = (bf16[2,32,896]{2,1,0:T(8,128)(2,1)S(1)}, bf16[2,32,896]{2,1,0:T(8,128)(2,1)S(1)}, u32[]{:S(2)}, u32[]{:S(2)}) collective-permute-start(bf16[2,32,896]{2,1,0:T(8,128)(2,1)S(1)} %get-tuple-element.53), channel_id=1, source_target_pairs={{0,192},{1,25},{2,194},{3,27},{4,196},{5,29},{6,198},{7,31},{8,200... | collective-permute-start | bytes 344072 | tf_op jit(solution)/shard_map/ppermute | solution.py:47
  45.6 10.5 %collective-permute-start.6 = (bf16[2,32,896]{2,1,0:T(8,128)(2,1)S(1)}, bf16[2,32,896]{2,1,0:T(8,128)(2,1)S(1)}, u32[]{:S(2)}, u32[]{:S(2)}) collective-permute-start(bf16[2,32,896]{2,1,0:T(8,128)(2,1)S(1)} %sum4.2.refs_1_), channel_id=1, source_target_pairs={{0,32},{1,33},{2,34},{3,35},{4,36},{5,37},{6,38},{7,39},{8,40},{9,... | collective-permute-start | bytes 344072 | tf_op jit(solution)/shard_map/ppermute | solution.py:51
  52.0 9.2 %collective-permute-start.13 = (bf16[2,32,896]{2,1,0:T(8,128)(2,1)S(1)}, bf16[2,32,896]{2,1,0:T(8,128)(2,1)S(1)}, u32[]{:S(2)}, u32[]{:S(2)}) collective-permute-start(bf16[2,32,896]{2,1,0:T(8,128)(2,1)S(1)} %sum4.3.refs_3_.refs_1_), channel_id=1, source_target_pairs={{0,32},{1,33},{2,34},{3,35},{4,36},{5,37},{6,38},{7,39},{8,40},{9,... | collective-permute-start | bytes 344072 | tf_op jit(solution)/shard_map/ppermute | solution.py:51
  56.7 9.2 %collective-permute-start.12 = (bf16[2,32,896]{2,1,0:T(8,128)(2,1)S(1)}, bf16[2,32,896]{2,1,0:T(8,128)(2,1)S(1)}, u32[]{:S(2)}, u32[]{:S(2)}) collective-permute-start(bf16[2,32,896]{2,1,0:T(8,128)(2,1)S(1)} %add2.2.refs_1_), channel_id=1, source_target_pairs={{0,192},{1,25},{2,194},{3,27},{4,196},{5,29},{6,198},{7,31},{8,200... | collective-permute-start | bytes 344072 | tf_op jit(solution)/shard_map/ppermute | solution.py:47
  59.4 7.5 %collective-permute-start.11 = (bf16[2,32,896]{2,1,0:T(8,128)(2,1)S(1)}, bf16[2,32,896]{2,1,0:T(8,128)(2,1)S(1)}, u32[]{:S(2)}, u32[]{:S(2)}) collective-permute-start(bf16[2,32,896]{2,1,0:T(8,128)(2,1)S(1)} %add2.2.refs_1_), channel_id=1, source_target_pairs={{0,128},{1,17},{2,130},{3,19},{4,132},{5,21},{6,134},{7,23},{8,136... | collective-permute-start | bytes 344072 | tf_op jit(solution)/shard_map/ppermute | solution.py:47
  59.7 7.3 %collective-permute-start.10 = (bf16[2,32,896]{2,1,0:T(8,128)(2,1)S(1)}, bf16[2,32,896]{2,1,0:T(8,128)(2,1)S(1)}, u32[]{:S(2)}, u32[]{:S(2)}) collective-permute-start(bf16[2,32,896]{2,1,0:T(8,128)(2,1)S(1)} %add2.2.refs_1_), channel_id=1, source_target_pairs={{0,64},{1,9},{2,66},{3,11},{4,68},{5,13},{6,70},{7,15},{8,72},{9,1... | collective-permute-start | bytes 344072 | tf_op jit(solution)/shard_map/ppermute | solution.py:47
  61.8 5.4 %collective-permute-start.16 = (bf16[2,32,896]{2,1,0:T(8,128)(2,1)S(1)}, bf16[2,32,896]{2,1,0:T(8,128)(2,1)S(1)}, u32[]{:S(2)}, u32[]{:S(2)}) collective-permute-start(bf16[2,32,896]{2,1,0:T(8,128)(2,1)S(1)} %add2.3.refs_5_), channel_id=1, source_target_pairs={{0,192},{1,25},{2,194},{3,27},{4,196},{5,29},{6,198},{7,31},{8,200... | collective-permute-start | bytes 344072 | tf_op jit(solution)/shard_map/ppermute | solution.py:47
  64.9 6.3 %collective-permute-start.15 = (bf16[2,32,896]{2,1,0:T(8,128)(2,1)S(1)}, bf16[2,32,896]{2,1,0:T(8,128)(2,1)S(1)}, u32[]{:S(2)}, u32[]{:S(2)}) collective-permute-start(bf16[2,32,896]{2,1,0:T(8,128)(2,1)S(1)} %add2.3.refs_5_), channel_id=1, source_target_pairs={{0,128},{1,17},{2,130},{3,19},{4,132},{5,21},{6,134},{7,23},{8,136... | collective-permute-start | bytes 344072 | tf_op jit(solution)/shard_map/ppermute | solution.py:47
  66.0 6.7 %collective-permute-start.14 = (bf16[2,32,896]{2,1,0:T(8,128)(2,1)S(1)}, bf16[2,32,896]{2,1,0:T(8,128)(2,1)S(1)}, u32[]{:S(2)}, u32[]{:S(2)}) collective-permute-start(bf16[2,32,896]{2,1,0:T(8,128)(2,1)S(1)} %add2.3.refs_5_), channel_id=1, source_target_pairs={{0,64},{1,9},{2,66},{3,11},{4,68},{5,13},{6,70},{7,15},{8,72},{9,1... | collective-permute-start | bytes 344072 | tf_op jit(solution)/shard_map/ppermute | solution.py:47
  73.3 14.7 %collective-permute-start.22 = (bf16[2,128,896]{2,1,0:T(8,128)(2,1)S(1)}, bf16[2,128,896]{2,1,0:T(8,128)(2,1)S(1)}, u32[]{:S(2)}, u32[]{:S(2)}) collective-permute-start(bf16[2,128,896]{2,1,0:T(8,128)(2,1)S(1)} %get-tuple-element.55.c0), channel_id=1, source_target_pairs={{0,24},{1,193},{2,26},{3,195},{4,28},{5,197},{6,30},{7,199},{8,0},... | collective-permute-start | bytes 1376264 | tf_op jit(solution)/shard_map/ppermute | solution.py:47
  73.8 14.2 %collective-permute-start.21 = (bf16[2,128,896]{2,1,0:T(8,128)(2,1)S(1)}, bf16[2,128,896]{2,1,0:T(8,128)(2,1)S(1)}, u32[]{:S(2)}, u32[]{:S(2)}) collective-permute-start(bf16[2,128,896]{2,1,0:T(8,128)(2,1)S(1)} %get-tuple-element.55.c0), channel_id=1, source_target_pairs={{0,16},{1,129},{2,18},{3,131},{4,20},{5,133},{6,22},{7,135},{8,24}... | collective-permute-start | bytes 1376264 | tf_op jit(solution)/shard_map/ppermute | solution.py:47
  75.5 13.3 %collective-permute-start.20 = (bf16[2,128,896]{2,1,0:T(8,128)(2,1)S(1)}, bf16[2,128,896]{2,1,0:T(8,128)(2,1)S(1)}, u32[]{:S(2)}, u32[]{:S(2)}) collective-permute-start(bf16[2,128,896]{2,1,0:T(8,128)(2,1)S(1)} %get-tuple-element.55.c0), channel_id=1, source_target_pairs={{0,8},{1,65},{2,10},{3,67},{4,12},{5,69},{6,14},{7,71},{8,16},{9,7... | collective-permute-start | bytes 1376264 | tf_op jit(solution)/shard_map/ppermute | solution.py:47
  77.3 22.3 %collective-permute-start.19 = (bf16[2,128,896]{2,1,0:T(8,128)(2,1)S(1)}, bf16[2,128,896]{2,1,0:T(8,128)(2,1)S(1)}, u32[]{:S(2)}, u32[]{:S(2)}) collective-permute-start(bf16[2,128,896]{2,1,0:T(8,128)(2,1)S(1)} %get-tuple-element.54.c0), channel_id=1, source_target_pairs={{0,24},{1,193},{2,26},{3,195},{4,28},{5,197},{6,30},{7,199},{8,0},... | collective-permute-start | bytes 1376264 | tf_op jit(solution)/shard_map/ppermute | solution.py:47
  77.5 22.0 %collective-permute-start.18 = (bf16[2,128,896]{2,1,0:T(8,128)(2,1)S(1)}, bf16[2,128,896]{2,1,0:T(8,128)(2,1)S(1)}, u32[]{:S(2)}, u32[]{:S(2)}) collective-permute-start(bf16[2,128,896]{2,1,0:T(8,128)(2,1)S(1)} %get-tuple-element.54.c0), channel_id=1, source_target_pairs={{0,16},{1,129},{2,18},{3,131},{4,20},{5,133},{6,22},{7,135},{8,24}... | collective-permute-start | bytes 1376264 | tf_op jit(solution)/shard_map/ppermute | solution.py:47
  88.0 11.6 %collective-permute-start.17 = (bf16[2,128,896]{2,1,0:T(8,128)(2,1)S(1)}, bf16[2,128,896]{2,1,0:T(8,128)(2,1)S(1)}, u32[]{:S(2)}, u32[]{:S(2)}) collective-permute-start(bf16[2,128,896]{2,1,0:T(8,128)(2,1)S(1)} %get-tuple-element.54.c0), channel_id=1, source_target_pairs={{0,8},{1,65},{2,10},{3,67},{4,12},{5,69},{6,14},{7,71},{8,16},{9,7... | collective-permute-start | bytes 1376264 | tf_op jit(solution)/shard_map/ppermute | solution.py:47
  111.2 14.0 %collective-permute-start.23 = (bf16[512,512]{1,0:T(8,128)(2,1)S(1)}, bf16[512,512]{1,0:T(8,128)(2,1)S(1)}, u32[]{:S(2)}, u32[]{:S(2)}) collective-permute-start(bf16[512,512]{1,0:T(8,128)(2,1)S(1)} %get-tuple-element.58), channel_id=1, source_target_pairs={{0,1},{1,0},{2,3},{3,2},{4,5},{5,4},{6,7},{7,6},{8,9},{9,8},{10,11... | collective-permute-start | bytes 1572872 | tf_op jit(solution)/shard_map/ppermute | solution.py:307
  111.5 13.6 %collective-permute-start.26 = (bf16[2,128,896]{2,1,0:T(8,128)(2,1)S(1)}, bf16[2,128,896]{2,1,0:T(8,128)(2,1)S(1)}, u32[]{:S(2)}, u32[]{:S(2)}) collective-permute-start(bf16[2,128,896]{2,1,0:T(8,128)(2,1)S(1)} %get-tuple-element.64), channel_id=1, source_target_pairs={{0,8},{1,65},{2,10},{3,67},{4,12},{5,69},{6,14},{7,71},{8,16},{9,7... | collective-permute-start | bytes 1376264 | tf_op jit(solution)/shard_map/ppermute | solution.py:47
  114.2 16.1 %collective-permute-start.27 = (bf16[2,128,896]{2,1,0:T(8,128)(2,1)S(1)}, bf16[2,128,896]{2,1,0:T(8,128)(2,1)S(1)}, u32[]{:S(2)}, u32[]{:S(2)}) collective-permute-start(bf16[2,128,896]{2,1,0:T(8,128)(2,1)S(1)} %get-tuple-element.65), channel_id=1, source_target_pairs={{0,16},{1,129},{2,18},{3,131},{4,20},{5,133},{6,22},{7,135},{8,24}... | collective-permute-start | bytes 1376264 | tf_op jit(solution)/shard_map/ppermute | solution.py:47
  114.8 20.1 %collective-permute-start.28 = (bf16[2,128,896]{2,1,0:T(8,128)(2,1)S(1)}, bf16[2,128,896]{2,1,0:T(8,128)(2,1)S(1)}, u32[]{:S(2)}, u32[]{:S(2)}) collective-permute-start(bf16[2,128,896]{2,1,0:T(8,128)(2,1)S(1)} %get-tuple-element.66), channel_id=1, source_target_pairs={{0,24},{1,193},{2,26},{3,195},{4,28},{5,197},{6,30},{7,199},{8,0},... | collective-permute-start | bytes 1376264 | tf_op jit(solution)/shard_map/ppermute | solution.py:47
  115.2 24.7 %collective-permute-start.29 = (bf16[2,128,896]{2,1,0:T(8,128)(2,1)S(1)}, bf16[2,128,896]{2,1,0:T(8,128)(2,1)S(1)}, u32[]{:S(2)}, u32[]{:S(2)}) collective-permute-start(bf16[2,128,896]{2,1,0:T(8,128)(2,1)S(1)} %get-tuple-element.72), channel_id=1, source_target_pairs={{0,8},{1,65},{2,10},{3,67},{4,12},{5,69},{6,14},{7,71},{8,16},{9,7... | collective-permute-start | bytes 1376264 | tf_op jit(solution)/shard_map/ppermute | solution.py:47
  125.2 14.7 %collective-permute-start.30 = (bf16[2,128,896]{2,1,0:T(8,128)(2,1)S(1)}, bf16[2,128,896]{2,1,0:T(8,128)(2,1)S(1)}, u32[]{:S(2)}, u32[]{:S(2)}) collective-permute-start(bf16[2,128,896]{2,1,0:T(8,128)(2,1)S(1)} %get-tuple-element.73), channel_id=1, source_target_pairs={{0,16},{1,129},{2,18},{3,131},{4,20},{5,133},{6,22},{7,135},{8,24}... | collective-permute-start | bytes 1376264 | tf_op jit(solution)/shard_map/ppermute | solution.py:47
  125.2 14.9 %collective-permute-start.31 = (bf16[2,128,896]{2,1,0:T(8,128)(2,1)S(1)}, bf16[2,128,896]{2,1,0:T(8,128)(2,1)S(1)}, u32[]{:S(2)}, u32[]{:S(2)}) collective-permute-start(bf16[2,128,896]{2,1,0:T(8,128)(2,1)S(1)} %get-tuple-element.74), channel_id=1, source_target_pairs={{0,24},{1,193},{2,26},{3,195},{4,28},{5,197},{6,30},{7,199},{8,0},... | collective-permute-start | bytes 1376264 | tf_op jit(solution)/shard_map/ppermute | solution.py:47
  130.4 8.9 %collective-permute-start.24 = (bf16[256,512]{1,0:T(8,128)(2,1)S(1)}, bf16[256,512]{1,0:T(8,128)(2,1)S(1)}, u32[]{:S(2)}, u32[]{:S(2)}) collective-permute-start(bf16[256,512]{1,0:T(8,128)(2,1)S(1)} %get-tuple-element.60), channel_id=1, source_target_pairs={{0,2},{1,3},{2,0},{3,1},{4,6},{5,7},{6,4},{7,5},{8,10},{9,11},{10,... | collective-permute-start | bytes 786440 | tf_op jit(solution)/shard_map/ppermute | solution.py:311
  140.9 9.8 %collective-permute-start.32 = (bf16[2,32,1792]{2,1,0:T(8,128)(2,1)S(1)}, bf16[2,32,1792]{2,1,0:T(8,128)(2,1)S(1)}, u32[]{:S(2)}, u32[]{:S(2)}) collective-permute-start(bf16[2,32,1792]{2,1,0:T(8,128)(2,1)S(1)} %get-tuple-element.76), channel_id=1, source_target_pairs={{0,64},{1,9},{2,66},{3,11},{4,68},{5,13},{6,70},{7,15},{8,72},{9,1... | collective-permute-start | bytes 688136 | tf_op jit(solution)/shard_map/ppermute | solution.py:47
  140.9 9.7 %collective-permute-start.33 = (bf16[2,32,1792]{2,1,0:T(8,128)(2,1)S(1)}, bf16[2,32,1792]{2,1,0:T(8,128)(2,1)S(1)}, u32[]{:S(2)}, u32[]{:S(2)}) collective-permute-start(bf16[2,32,1792]{2,1,0:T(8,128)(2,1)S(1)} %get-tuple-element.77), channel_id=1, source_target_pairs={{0,128},{1,17},{2,130},{3,19},{4,132},{5,21},{6,134},{7,23},{8,136... | collective-permute-start | bytes 688136 | tf_op jit(solution)/shard_map/ppermute | solution.py:47
  143.3 8.3 %collective-permute-start.34 = (bf16[2,32,1792]{2,1,0:T(8,128)(2,1)S(1)}, bf16[2,32,1792]{2,1,0:T(8,128)(2,1)S(1)}, u32[]{:S(2)}, u32[]{:S(2)}) collective-permute-start(bf16[2,32,1792]{2,1,0:T(8,128)(2,1)S(1)} %get-tuple-element.78), channel_id=1, source_target_pairs={{0,192},{1,25},{2,194},{3,27},{4,196},{5,29},{6,198},{7,31},{8,200... | collective-permute-start | bytes 688136 | tf_op jit(solution)/shard_map/ppermute | solution.py:47
  144.4 19.7 %collective-permute-start.25 = (bf16[128,512]{1,0:T(8,128)(2,1)S(1)}, bf16[128,512]{1,0:T(8,128)(2,1)S(1)}, u32[]{:S(2)}, u32[]{:S(2)}) collective-permute-start(bf16[128,512]{1,0:T(8,128)(2,1)S(1)} %get-tuple-element.62), channel_id=1, source_target_pairs={{0,4},{1,5},{2,6},{3,7},{4,0},{5,1},{6,2},{7,3},{8,12},{9,13},{10,... | collective-permute-start | bytes 393224 | tf_op jit(solution)/shard_map/ppermute | solution.py:311
  152.2 15.9 %collective-permute-start.35 = (bf16[2,16,1792]{2,1,0:T(8,128)(2,1)S(1)}, bf16[2,16,1792]{2,1,0:T(8,128)(2,1)S(1)}, u32[]{:S(2)}, u32[]{:S(2)}) collective-permute-start(bf16[2,16,1792]{2,1,0:T(8,128)(2,1)S(1)} %get-tuple-element.80), channel_id=1, source_target_pairs={{0,32},{1,33},{2,34},{3,35},{4,36},{5,37},{6,38},{7,39},{8,40},{9,... | collective-permute-start | bytes 344072 | tf_op jit(solution)/shard_map/ppermute | solution.py:51
